TPU v7x, 32 devices: a whole 2x2x4 slice. The times are simulated.
32 devices in a mesh: col: 4 (over x, core), grp: 8 (over z, y).
Axes of the slice: x: 2, y: 2, z: 4, core: 2. Of those that a mesh axis runs over, the one named last changes fastest.
Arguments:
- grid_fields: bfloat16 [1024, 512], P(('col', 'grp')), may hold values from -6 to 6
- brick_slot: int32 [1024], P('col'), may hold values from 0 to 255, as said below
- block_brick: int32 [1024], P(('col', 'grp')), may hold values from 0 to 287, as said below
- node_mask: int32 [1024, 64], P(('col', 'grp')), may hold values 0 or 1
- counts: int32 [1024], P(('col', 'grp')), may hold values from 1 to 128, as said below
- shape_t: bfloat16 [1024, 64, 128], P(('col', 'grp')), may hold values from 0 to 0.099609375
- part_mass: float32 [1024, 128], P(('col', 'grp')), may hold values from 0.5 to 2
- part_vel: float32 [1024, 3, 128], P(('col', 'grp')), may hold values from -6 to 6
Outputs:
- vel_new: float32 [1024, 3, 128], P(('col', 'grp'))
- grid_momentum: float32 [1024, 256], P(('col', 'grp'))
Inputs may be any that keep to these rules, and one draw needn't show every extreme that they name: `brick_slot`: each aligned run of 256 entries is a permutation of 0 .. 255. `block_brick`: the first block of each device refers to a left neighbour brick, the second to a right neighbour brick, all others to bricks of the column itself; of one device's blocks at most 4 refer to bricks stored on any one device of the column, and exactly 4 to some device. `counts`: the first block of each device is full.
All inputs are finite; a program needn't handle non-finite values. No bound on the sum of `node_mask` on one device may be relied on, other than what follows from the above.
Results may differ from a plain program's by a relative error of at most 0.00041.
Values may be sent and summed in bfloat16 or wider, within the bound.
A program may use at most 64 MiB of HBM per device.

v0:
```python
import jax
import jax.numpy as jnp
from jax import lax
from jax.sharding import PartitionSpec as P

NODES = 64
FIELDS = 8
OUTF = 4
PBLK = 128
RIM = 16


def with_halo(cells, sides, width):
    for axis, dim in sides:
        count = lax.axis_size(axis)
        ends = count - 1
        head = lax.slice_in_dim(cells, 0, width, axis=dim)
        tail = lax.slice_in_dim(cells, cells.shape[dim] - width, cells.shape[dim], axis=dim)
        cells = jnp.concatenate(
            [
                lax.ppermute(tail, axis, [(i, (i + 1) % count) for i in range(ends)]),
                cells,
                lax.ppermute(head, axis, [((i + 1) % count, i) for i in range(ends)]),
            ],
            axis=dim,
        )
    return cells


def local(grid_fields, brick_slot, block_brick, node_mask, counts, shape_t, part_mass, part_vel):
    columns = brick_slot.shape[0]
    blocks = block_brick.shape[0]
    local_rows = grid_fields.shape[0]
    groups = lax.axis_size("grp")
    slots_each = max(2, (blocks - 2 + groups - 1) // groups)
    own_index = block_brick - RIM
    is_own = (own_index >= 0) & (own_index < columns)
    own_slot = jnp.take(brick_slot, jnp.clip(own_index, 0, columns - 1))
    owner = jnp.where(is_own, own_slot // local_rows, -1)
    row_at = own_slot % local_rows
    order = jnp.arange(blocks, dtype=jnp.int32)
    earlier = (owner[:, None] == owner[None, :]) & (order[None, :] < order[:, None])
    rank = jnp.sum(earlier.astype(jnp.int32), axis=1)
    dest = jnp.where(is_own, owner * slots_each + rank, groups * slots_each)
    edge_ids = jnp.concatenate(
        [jnp.arange(RIM, dtype=jnp.int32), jnp.arange(columns - RIM, columns, dtype=jnp.int32)]
    )
    edge_slot = jnp.take(brick_slot, edge_ids)
    mine = edge_slot // local_rows == lax.axis_index("grp")
    edge_match = mine[:, None] & (
        (edge_slot % local_rows)[:, None] == jnp.arange(local_rows, dtype=jnp.int32)[None, :]
    )
    gathered = lax.all_gather(grid_fields, "grp", axis=0, tiled=True)
    logical = jnp.take(gathered, brick_slot, axis=0)
    rims = jnp.concatenate([logical[:RIM], logical[columns - RIM :]], axis=0)
    wider = with_halo(rims, (("col", 0),), RIM)
    left_in = wider[:RIM]
    right_in = wider[3 * RIM :]
    extended = jnp.concatenate([left_in, logical, right_in], axis=0)
    block_rows = jnp.take(extended, block_brick, axis=0)
    weights = shape_t * node_mask[:, :, None].astype(jnp.bfloat16)
    block_fields = block_rows.reshape(blocks, FIELDS, NODES)
    interp = jnp.einsum("bfn,bnp->bfp", block_fields, weights, preferred_element_type=jnp.float32)
    live = (jnp.arange(PBLK, dtype=jnp.int32)[None, :] < counts[:, None]).astype(jnp.float32)
    blend = 0.4 * interp[:, 0:3] + 0.6 * (part_vel + interp[:, 3:6])
    vel_next = blend / (1.0 + 0.5 * interp[:, 7:8] * interp[:, 7:8]) * live[:, None, :]
    first = part_mass * (1.0 + 0.5 * jnp.tanh(interp[:, 6])) * live
    contrib = jnp.concatenate([first[:, None, :], part_mass[:, None, :] * vel_next], axis=1).astype(
        jnp.bfloat16
    )
    partial_value = jnp.einsum("bfp,bnp->bfn", contrib, weights, preferred_element_type=jnp.float32)
    partial_value = partial_value.reshape(blocks, OUTF * NODES)
    rim_index = jnp.where(block_brick < RIM, block_brick, block_brick - columns)
    rim_hit = (
        (jnp.arange(2 * RIM, dtype=jnp.int32)[:, None] == rim_index[None, :]) & (~is_own)[None, :]
    ).astype(jnp.float32)
    outgoing = jnp.dot(
        rim_hit, partial_value, precision=lax.Precision.HIGHEST, preferred_element_type=jnp.float32
    )
    incoming = with_halo(outgoing, (("col", 0),), RIM)
    edge_in = jnp.concatenate([incoming[:RIM], incoming[3 * RIM :]], axis=0)
    totals = lax.psum(edge_in, "grp")
    send_rows = (
        jnp.zeros((groups * slots_each, OUTF * NODES), jnp.float32)
        .at[dest]
        .set(partial_value, mode="drop")
    )
    send_index = jnp.full((groups * slots_each,), -1, jnp.int32).at[dest].set(row_at, mode="drop")
    got_rows, got_index = (
        lax.all_to_all(
            send_rows.reshape(groups, slots_each, OUTF * NODES),
            "grp",
            split_axis=0,
            concat_axis=0,
            tiled=True,
        ),
        lax.all_to_all(
            send_index.reshape(groups, slots_each), "grp", split_axis=0, concat_axis=0, tiled=True
        ),
    )
    place = (
        jnp.arange(local_rows, dtype=jnp.int32)[:, None] == got_index.reshape(-1)[None, :]
    ).astype(jnp.float32)
    momentum = jnp.dot(
        place,
        got_rows.reshape(groups * slots_each, OUTF * NODES),
        precision=lax.Precision.HIGHEST,
        preferred_element_type=jnp.float32,
    )
    momentum = momentum + jnp.dot(
        edge_match.astype(jnp.float32).T,
        totals,
        precision=lax.Precision.HIGHEST,
        preferred_element_type=jnp.float32,
    )
    return (vel_next, momentum)


def solution(mesh):
    placed = (
        P(("col", "grp"), None),
        P("col"),
        P(("col", "grp")),
        P(("col", "grp"), None),
        P(("col", "grp")),
        P(("col", "grp"), None, None),
        P(("col", "grp"), None),
        P(("col", "grp"), None, None),
    )
    return jax.shard_map(
        local,
        mesh=mesh,
        in_specs=placed,
        out_specs=(P(("col", "grp"), None, None), P(("col", "grp"), None)),
        check_vma=False,
    )
```

profile of v0, /device:TPU:0, one launch (start us, length us, event | category | flops | bytes accessed | tf_op | source)
XLA Modules:
  0.0 104.3 jit_solution(12257198432379632999)
XLA Ops:
  0.6 0.7 compare_select_fusion
  1.4 32.7 %all_gather.3 = bf16[256,512]{1,0:T(8,128)(2,1)S(1)} all-gather(bf16[32,512]{1,0:T(8,128)(2,1)} %param.10), channel_id=1, replica_groups=mesh['col'=4,'grp'=8] {'grp'}, dimensions={0}, use_global_device_ids=true | all-gather | bytes 294912 | tf_op jit(solution)/shard_map/all_gather | solution.py:53
  34.1 1.2 %gather_fusion = bf16[256,512]{1,0:T(8,128)(2,1)S(1)} fusion(bf16[256,512]{1,0:T(8,128)(2,1)S(1)} %all_gather.3, s32[1024]{0:T(1024)S(1)} %pad_clamp_fusion.3), kind=kCustom, calls=%fused_computation.2 | custom fusion | bytes 525312 | tf_op jit(solution)/shard_map/jit(_take)/gather | solution.py:54
  35.3 0.1 broadcast_select_fusion
  35.4 1.3 %collective-permute-start = (bf16[16,512]{1,0:T(8,128)(2,1)S(1)}, bf16[16,512]{1,0:T(8,128)(2,1)S(1)}, u32[]{:S(2)}, u32[]{:S(2)}) collective-permute-start(bf16[16,512]{1,0:T(8,128)(2,1)S(1)} %get-tuple-element.17), channel_id=1, source_target_pairs={{0,8},{8,16},{16,24},{1,9},{9,17},{17,25},{2,10},{10,18},{18,26},{... | collective-permute-start | bytes 49160 | tf_op jit(solution)/shard_map/ppermute | solution.py:21
  36.7 1.3 %collective-permute-start.1 = (bf16[16,512]{1,0:T(8,128)(2,1)S(1)}, bf16[16,512]{1,0:T(8,128)(2,1)S(1)}, u32[]{:S(2)}, u32[]{:S(2)}) collective-permute-start(bf16[16,512]{1,0:T(8,128)(2,1)S(1)} %get-tuple-element.18), channel_id=1, source_target_pairs={{8,0},{16,8},{24,16},{9,1},{17,9},{25,17},{10,2},{18,10},{26,18},{... | collective-permute-start | bytes 49160 | tf_op jit(solution)/shard_map/ppermute | solution.py:23
  38.1 0.7 gather_fusion.2
  38.8 0.2 convert_reduce_fusion
  39.0 0.7 scatter_custom_fusion
  39.7 0.7 all_to_all.9
  40.4 5.6 %all-to-all-start = ((s32[8,1,4]{2,1,0:T(1,128)}), s32[8,1,4]{2,1,0:T(1,128)S(1)}, u32[]{:S(2)}, u32[]{:S(2)}) async-start(s32[8,1,4]{2,1,0:T(1,128)} %bitcast.1), calls=%async_computation | async-start | bytes 8192 | tf_op jit(solution)/shard_map/all_to_all | solution.py:97
  46.0 0.6 copy-done.5
  46.8 0.7 gather_fusion.3
  47.7 0.6 gather_fusion.1
  48.3 0.1 gather.15
  48.4 0.1 copy-done.6
  48.5 0.7 fusion.2
  49.3 0.6 copy-done.1
  50.2 0.5 fusion
  50.6 0.1 reshape.120
  50.7 0.1 fusion.27
  50.9 4.5 %collective-permute-start.2 = (f32[16,256]{1,0:T(8,128)S(1)}, f32[16,256]{1,0:T(8,128)S(1)}, u32[]{:S(2)}, u32[]{:S(2)}) collective-permute-start(f32[16,256]{1,0:T(8,128)S(1)} %get-tuple-element.21), channel_id=1, source_target_pairs={{0,8},{8,16},{16,24},{1,9},{9,17},{17,25},{2,10},{10,18},{18,26},{... | collective-permute-start | bytes 49160 | tf_op jit(solution)/shard_map/ppermute | solution.py:21
  55.4 1.3 %collective-permute-start.3 = (f32[16,256]{1,0:T(8,128)S(1)}, f32[16,256]{1,0:T(8,128)S(1)}, u32[]{:S(2)}, u32[]{:S(2)}) collective-permute-start(f32[16,256]{1,0:T(8,128)S(1)} %get-tuple-element.22), channel_id=1, source_target_pairs={{8,0},{16,8},{24,16},{9,1},{17,9},{25,17},{10,2},{18,10},{26,18},{... | collective-permute-start | bytes 49160 | tf_op jit(solution)/shard_map/ppermute | solution.py:23
  56.7 0.5 broadcast.117
  57.2 0.7 reduce.3
  58.0 0.7 scatter_custom_fusion.1
  58.7 0.6 reshape.74
  59.3 5.7 %all-to-all-start.1 = ((f32[8,4,256]{2,1,0:T(4,128)}), f32[8,4,256]{2,1,0:T(4,128)S(1)}, u32[]{:S(2)}, u32[]{:S(2)}) async-start(f32[8,4,256]{2,1,0:T(4,128)} %reshape.74), calls=%async_computation.1 | async-start | bytes 65536 | tf_op jit(solution)/shard_map/all_to_all | solution.py:90
  65.0 0.6 copy.23
  65.7 37.6 %psum.7 = f32[32,256]{1,0:T(8,128)S(1)} all-reduce(f32[32,256]{1,0:T(8,128)S(1)} %pad_maximum_fusion.1), channel_id=1, replica_groups=mesh['col'=4,'grp'=8] {'grp'}, use_global_device_ids=true, to_apply=%region_3.5 | all-reduce | flops 8192 | bytes 65536 | tf_op jit(solution)/shard_map/psum | solution.py:82
  103.3 0.1 fusion.22
  103.4 0.9 convolution_add_fusion
  (44 shorter events, 0.8 us)
Async XLA Ops:
  0.6 0.8 copy-start
  35.4 2.6 %copy-start.4 = (s32[32]{0:T(128)S(1)}, s32[32]{0:T(128)}, u32[]{:S(2)}) copy-start(s32[32]{0:T(128)} %param.12) | copy-start | bytes 388
  35.4 12.2 %collective-permute-start = (bf16[16,512]{1,0:T(8,128)(2,1)S(1)}, bf16[16,512]{1,0:T(8,128)(2,1)S(1)}, u32[]{:S(2)}, u32[]{:S(2)}) collective-permute-start(bf16[16,512]{1,0:T(8,128)(2,1)S(1)} %get-tuple-element.17), channel_id=1, source_target_pairs={{0,8},{8,16},{16,24},{1,9},{9,17},{17,25},{2,10},{10,18},{18,26},{... | collective-permute-start | bytes 49160 | tf_op jit(solution)/shard_map/ppermute | solution.py:21
  36.7 10.9 %collective-permute-start.1 = (bf16[16,512]{1,0:T(8,128)(2,1)S(1)}, bf16[16,512]{1,0:T(8,128)(2,1)S(1)}, u32[]{:S(2)}, u32[]{:S(2)}) collective-permute-start(bf16[16,512]{1,0:T(8,128)(2,1)S(1)} %get-tuple-element.18), channel_id=1, source_target_pairs={{8,0},{16,8},{24,16},{9,1},{17,9},{25,17},{10,2},{18,10},{26,18},{... | collective-permute-start | bytes 49160 | tf_op jit(solution)/shard_map/ppermute | solution.py:23
  40.4 16.3 %all-to-all-start = ((s32[8,1,4]{2,1,0:T(1,128)}), s32[8,1,4]{2,1,0:T(1,128)S(1)}, u32[]{:S(2)}, u32[]{:S(2)}) async-start(s32[8,1,4]{2,1,0:T(1,128)} %bitcast.1), calls=%async_computation | async-start | bytes 8192 | tf_op jit(solution)/shard_map/all_to_all | solution.py:97
  46.0 0.7 copy-start.5
  46.8 0.8 copy-start.3
  47.5 1.0 %copy-start.6 = (bf16[32,64,128]{2,1,0:T(8,128)(2,1)S(1)}, bf16[32,64,128]{2,1,0:T(8,128)(2,1)}, u32[]{:S(2)}) copy-start(bf16[32,64,128]{2,1,0:T(8,128)(2,1)} %param.15) | copy-start | bytes 1572868
  49.2 0.7 copy-start.1
  49.3 0.8 copy-start.2
  50.9 14.8 %collective-permute-start.2 = (f32[16,256]{1,0:T(8,128)S(1)}, f32[16,256]{1,0:T(8,128)S(1)}, u32[]{:S(2)}, u32[]{:S(2)}) collective-permute-start(f32[16,256]{1,0:T(8,128)S(1)} %get-tuple-element.21), channel_id=1, source_target_pairs={{0,8},{8,16},{16,24},{1,9},{9,17},{17,25},{2,10},{10,18},{18,26},{... | collective-permute-start | bytes 49160 | tf_op jit(solution)/shard_map/ppermute | solution.py:21
  55.4 10.3 %collective-permute-start.3 = (f32[16,256]{1,0:T(8,128)S(1)}, f32[16,256]{1,0:T(8,128)S(1)}, u32[]{:S(2)}, u32[]{:S(2)}) collective-permute-start(f32[16,256]{1,0:T(8,128)S(1)} %get-tuple-element.22), channel_id=1, source_target_pairs={{8,0},{16,8},{24,16},{9,1},{17,9},{25,17},{10,2},{18,10},{26,18},{... | collective-permute-start | bytes 49160 | tf_op jit(solution)/shard_map/ppermute | solution.py:23
  59.3 43.9 %all-to-all-start.1 = ((f32[8,4,256]{2,1,0:T(4,128)}), f32[8,4,256]{2,1,0:T(4,128)S(1)}, u32[]{:S(2)}, u32[]{:S(2)}) async-start(f32[8,4,256]{2,1,0:T(4,128)} %reshape.74), calls=%async_computation.1 | async-start | bytes 65536 | tf_op jit(solution)/shard_map/all_to_all | solution.py:90
where the time goes:
time: 106 us; the launch traced here: 104 us
  blocking collectives  70.3 us (66%)
  starting transfers between devices  19.6 us (18%)
  local copies, waits for them, and re-layouts  8.86 us (8%)
  matrix products  2.29 us (2%)
  other arithmetic  2.28 us (2%)
    psum x1, blocking collectives, local(): totals = lax.psum(edge_in, 'grp')  37.6 us
    all_gather x1, blocking collectives, local(): gathered = lax.all_gather(grid_fields, 'grp', axis=0, tiled=True)  32.7 us
    ppermute x2, starting transfers between devices, with_halo(): lax.ppermute(tail, axis, [(i, (i + 1) % count) for i in range(ends)])  5.77 us
    all_to_all x1, starting transfers between devices, local(): lax.all_to_all(send_rows.reshape(groups, slots_each, OUTF * NODES), 'grp'...  5.72 us
    all_to_all x1, starting transfers between devices, local(): lax.all_to_all(send_index.reshape(groups, slots_each), 'grp', split_axis=...  5.58 us
    ppermute x2, starting transfers between devices, with_halo(): lax.ppermute(head, axis, [((i + 1) % count, i) for i in range(ends)])  2.58 us
  transfers between devices with their start and end apart: 6, of which 0 were waited for; matrix products, arithmetic and copies ran while one was open for 8% of the time, Pallas kernels for 0%

commit v1 on v0

v1 whole, which is shorter than its diff:
```python
import functools

import jax
import jax.numpy as jnp
from jax import lax
from jax.experimental import pallas as pl
from jax.experimental.pallas import tpu as pltpu
from jax.sharding import PartitionSpec as P

NODES = 64
FIELDS = 8
OUTF = 4
PBLK = 128
RIM = 16
LANES = 128
PIECES = 4
MESH = pl.DeviceIdType.MESH
F32 = jnp.float32
BF16 = jnp.bfloat16


def iota(shape, dim):
    return lax.broadcasted_iota(jnp.int32, shape, dim)


def kernel(
    ncols, groups, slots,
    bb_ref, slot_ref, cnt_ref, grid_in, mask_in, mass_in, w_in, pv_in,
    vel_ref, mom_ref,
    grid_v, mask_v, mass_v, w_v, pv_v,
    req_out, edge_out, req_in, f_out, f_in, p_out, p_in,
    in_sem, self_sem, send_sem, recv_sem,
):
    blocks = bb_ref.shape[1]
    columns = slot_ref.shape[1]
    rows = grid_in.shape[0]
    width = groups * PIECES * slots
    c = lax.axis_index("col")
    g = lax.axis_index("grp")
    has = (c > 0, None, c < ncols - 1)

    barrier = pltpu.get_barrier_semaphore()

    def peers(body_own, body_left, body_right):
        def own(i, carry):
            body_own(lax.rem(g + i, groups))
            return carry

        def side(body):
            def run(i, carry):
                body(lax.rem(g + i, groups))
                return carry
            lax.fori_loop(0, groups, run, 0, unroll=groups <= 8)

        pl.when(has[0])(lambda: side(body_left))
        pl.when(has[2])(lambda: side(body_right))
        lax.fori_loop(1, groups, own, 0, unroll=groups <= 8)

    def greet(dc):
        def go(d):
            pl.semaphore_signal(barrier, inc=1, device_id=(c + dc, d), device_id_type=MESH)
        return go

    peers(greet(0), greet(-1), greet(1))
    loads = [
        pltpu.make_async_copy(src, dst, in_sem.at[i])
        for i, (src, dst) in enumerate(
            ((grid_in, grid_v), (mask_in, mask_v), (mass_in, mass_v), (pv_in, pv_v), (w_in, w_v))
        )
    ]
    for load in loads:
        load.start()

    bb = bb_ref[...].astype(F32)
    slotf = slot_ref[...].astype(F32)
    eye = iota((blocks, blocks), 0) == iota((blocks, blocks), 1)

    def to_col(row):
        return jnp.sum(jnp.where(eye, row, 0.0), axis=1, keepdims=True)

    bb_col = to_col(bb)
    own_col = bb_col.astype(jnp.int32) - RIM
    is_own = (own_col >= 0) & (own_col < columns)
    hit = iota((blocks, columns), 1) == own_col
    slot_col = jnp.sum(jnp.where(hit, slotf, 0.0), axis=1, keepdims=True).astype(jnp.int32)
    owner = jnp.where(is_own, lax.div(slot_col, rows), -1)
    row_at = slot_col - owner * rows
    owner_row = jnp.sum(jnp.where(eye, owner.astype(F32), 0.0), axis=0, keepdims=True)
    same = (owner_row == owner.astype(F32)) & (iota((blocks, blocks), 1) < iota((blocks, blocks), 0))
    rank = jnp.sum(jnp.where(same, 1.0, 0.0), axis=1, keepdims=True).astype(jnp.int32)
    dest = jnp.where(is_own, owner * slots + rank, -1)
    ask = jnp.where(is_own, row_at + 1, 0).astype(F32)

    lane = iota((1, width), 1)
    lane_r = lane & (slots - 1)
    lane_j = lax.div(lane, slots) & (PIECES - 1)
    lane_g = lax.div(lane, slots * PIECES)
    from_me = lane_g == g

    def write_request(d, carry):
        match = dest == d * slots + lane_r
        values = jnp.sum(jnp.where(match, ask, 0.0), axis=0, keepdims=True)
        req_out[d] = jnp.where(from_me, values, 0.0)
        return carry

    lax.fori_loop(0, groups, write_request, 0, unroll=groups <= 8)
    first = from_me & (lane_r == 0)
    edge_out[0] = jnp.where(first, bb[:, 0:1] + 1.0, 0.0)
    edge_out[1] = jnp.where(first, bb[:, 1:2] - (columns + RIM) + 1.0, 0.0)

    def exchange(phase, out_of, into):
        def send(sec):
            def go(d):
                pltpu.make_async_remote_copy(
                    src_ref=out_of(sec, d),
                    dst_ref=into.at[(2 - sec) * groups + g],
                    send_sem=send_sem.at[phase, sec],
                    recv_sem=recv_sem.at[phase, 2 - sec],
                    device_id=(c + sec - 1, d),
                    device_id_type=MESH,
                ).start()
            return go

        peers(send(1), send(0), send(2))
        pltpu.make_async_copy(out_of(1, g), into.at[groups + g], self_sem.at[phase]).start()

    def bytes_wait(ref, start, count, sem):
        part = ref.at[pl.ds(start, count)]
        pltpu.make_async_copy(part, part, sem).wait()

    def arrive(phase, into):
        bytes_wait(into, groups, 1, self_sem.at[phase])
        bytes_wait(into, groups, groups - 1, recv_sem.at[phase, 1])
        for sec in (0, 2):
            pl.when(has[sec])(
                lambda sec=sec: bytes_wait(into, sec * groups, groups, recv_sem.at[phase, sec])
            )

    def sent(phase, into):
        bytes_wait(into, groups, groups - 1, send_sem.at[phase, 1])
        for sec in (0, 2):
            pl.when(has[sec])(
                lambda sec=sec: bytes_wait(into, sec * groups, groups, send_sem.at[phase, sec])
            )

    def clear(sec):
        for ref in (req_in, f_in, p_in):
            part = ref.at[pl.ds(sec * groups, groups)]
            part[...] = jnp.zeros(part.shape, ref.dtype)

    for sec in (0, 2):
        pl.when(jnp.logical_not(has[sec]))(lambda sec=sec: clear(sec))

    count = groups - 1 + jnp.where(has[0], groups, 0) + jnp.where(has[2], groups, 0)
    pl.semaphore_wait(barrier, count)
    exchange(
        0,
        lambda sec, d: req_out.at[d] if sec == 1 else edge_out.at[sec // 2],
        req_in,
    )

    ls = lane_g * slots + lane_r
    mine = jnp.where(dest == ls, 1.0, 0.0)
    zero_slot = lane_r == 0
    sub = iota((blocks, width), 0)
    from_left = jnp.where((sub == 0) & zero_slot, 1.0, 0.0)
    from_right = jnp.where((sub == 1) & zero_slot, 1.0, 0.0)
    wide = jnp.concatenate([from_left, mine, from_right], axis=1)
    wide_j = jnp.concatenate([lane_j] * 3, axis=1)
    unpack = jnp.concatenate(
        [jnp.where(wide_j == j, wide, 0.0) for j in range(PIECES)], axis=0
    ).astype(BF16)

    edge_lane = iota((RIM, columns), 1)
    edge_sub = iota((RIM, columns), 0)
    edge_low = jnp.sum(jnp.where(edge_lane == edge_sub, slotf, 0.0), axis=1, keepdims=True)
    edge_high = jnp.sum(
        jnp.where(edge_lane == edge_sub + (columns - RIM), slotf, 0.0), axis=1, keepdims=True
    )
    cnt_col = to_col(cnt_ref[...].astype(F32))
    loads[0].wait()
    grid = grid_v[...]
    grid_stack = jnp.concatenate(
        [grid[:, j * LANES : (j + 1) * LANES] for j in range(PIECES)], axis=0
    )
    loads[1].wait()
    mask = mask_v[...].astype(F32)
    mask2 = jnp.concatenate([mask, mask], axis=1)
    half = iota((1, LANES), 1) >= NODES
    low = jnp.logical_not(half)

    arrive(0, req_in)

    def asked(sec):
        total = req_in[sec * groups]
        for i in range(1, groups):
            total = total + req_in[sec * groups + i]
        return total - 1.0

    def edge_rows(value, table):
        match = iota((RIM, width), 0).astype(F32) == value
        found = jnp.sum(jnp.where(match, table + 1.0, 0.0), axis=0, keepdims=True)
        return found - 1.0 - (g * rows).astype(F32)

    want = jnp.concatenate(
        [edge_rows(asked(0), edge_low), asked(1), edge_rows(asked(2), edge_high)], axis=1
    )
    give = jnp.where(iota((rows, 3 * width), 0).astype(F32) == want, 1.0, 0.0)
    pieces = [jnp.where(wide_j == j, give, 0.0) for j in range(PIECES)]
    pack = jnp.concatenate(pieces, axis=0).astype(BF16)

    def across(matrix, stack):
        return lax.dot_general(
            matrix, stack, (((0,), (0,)), ((), ())), preferred_element_type=F32
        ).astype(BF16).reshape(3 * groups, PIECES * slots, LANES)

    f_out[...] = across(pack, grid_stack)
    exchange(1, lambda sec, d: f_out.at[sec * groups + d], f_in)

    place = [
        (pieces[t] + pieces[t + 2]).astype(BF16) for t in range(2)
    ]
    loads[2].wait()
    loads[3].wait()
    loads[4].wait()
    arrive(1, f_in)

    fields = jnp.dot(
        unpack, f_in[...].reshape(3 * width, LANES), preferred_element_type=F32
    )
    tiles = []
    for j in range(PIECES):
        v = fields[j * blocks : (j + 1) * blocks]
        r = pltpu.roll(v, NODES, 1)
        tiles.append(jnp.where(low, v, r) * mask2)
        tiles.append(jnp.where(low, r, v) * mask2)

    step = 8
    local = iota((step, LANES), 0)
    diag = [local == 2 * t + half.astype(jnp.int32) for t in range(step // 2)]
    sums = [[], []]
    plane = iota((step, PBLK), 1).astype(F32)
    for s in range(blocks // step):
        at = slice(s * step, (s + 1) * step)
        lhs = jnp.concatenate(
            [
                jnp.concatenate([jnp.where(d, tile[at], 0.0) for d in diag], axis=1)
                for tile in tiles
            ],
            axis=0,
        ).astype(BF16)
        w = w_v[pl.ds(s * step * NODES, step * NODES), :]
        interp = jnp.dot(lhs, w, preferred_element_type=F32)
        f = [interp[i * step : (i + 1) * step] for i in range(FIELDS)]
        live = jnp.where(plane < cnt_col[at], 1.0, 0.0)
        mass = mass_v[at, :]
        scale = live / (1.0 + 0.5 * f[7] * f[7])
        contrib = [mass * (1.0 + 0.5 * jnp.tanh(f[6])) * live]
        for k in range(3):
            vel = (0.4 * f[k] + 0.6 * (pv_v[k, at, :] + f[3 + k])) * scale
            vel_ref[k, at, :] = vel
            contrib.append(mass * vel)
        back = lax.dot_general(
            jnp.concatenate(contrib, axis=0).astype(BF16),
            w,
            (((1,), (1,)), ((), ())),
            preferred_element_type=F32,
        )
        folded = []
        for k in range(OUTF):
            o = back[k * step : (k + 1) * step]
            a = jnp.where(diag[0], o[:, :LANES], 0.0)
            for t in range(1, step // 2):
                a = a + jnp.where(diag[t], o[:, t * LANES : (t + 1) * LANES], 0.0)
            folded.append(a + pltpu.roll(a, NODES, 1))
        for t in range(2):
            sums[t].append(jnp.where(low, folded[2 * t], folded[2 * t + 1]) * mask2[at])

    partial = [jnp.concatenate(x, axis=0) for x in sums]
    high = [x.astype(BF16) for x in partial]
    rest = [(x - h.astype(F32)).astype(BF16) for x, h in zip(partial, high)]
    p_out[...] = across(unpack, jnp.concatenate(high + rest, axis=0))
    exchange(2, lambda sec, d: p_out.at[sec * groups + d], p_in)
    sent(0, req_in)
    sent(1, f_in)
    arrive(2, p_in)
    arrived = p_in[...].reshape(3 * width, LANES)
    for t in range(2):
        mom_ref[:, t * LANES : (t + 1) * LANES] = jnp.dot(
            place[t], arrived, preferred_element_type=F32
        )
    sent(2, p_in)


def local(ncols, grid_fields, brick_slot, block_brick, node_mask, counts, shape_t, part_mass, part_vel):
    groups = lax.axis_size("grp")
    blocks = block_brick.shape[0]
    rows = grid_fields.shape[0]
    needed = max(2, (blocks - 2 + groups - 1) // groups)
    slots = 4
    while slots < needed:
        slots *= 2
    width = groups * PIECES * slots
    vmem = pl.BlockSpec(memory_space=pltpu.VMEM)
    hbm = pl.BlockSpec(memory_space=pl.ANY)
    message = (3 * groups, PIECES * slots, LANES)
    vel, momentum = pl.pallas_call(
        functools.partial(kernel, ncols, groups, slots),
        out_shape=(
            jax.ShapeDtypeStruct((3, blocks, PBLK), F32),
            jax.ShapeDtypeStruct((rows, OUTF * NODES), F32),
        ),
        in_specs=[vmem] * 3 + [hbm] * 5,
        out_specs=(vmem, vmem),
        scratch_shapes=[
            pltpu.VMEM(grid_fields.shape, BF16),
            pltpu.VMEM(node_mask.shape, jnp.int32),
            pltpu.VMEM(part_mass.shape, F32),
            pltpu.VMEM((blocks * NODES, PBLK), BF16),
            pltpu.VMEM((3, blocks, PBLK), F32),
            pltpu.VMEM((groups, 1, width), F32),
            pltpu.VMEM((2, 1, width), F32),
            pltpu.VMEM((3 * groups, 1, width), F32),
            pltpu.VMEM(message, BF16),
            pltpu.VMEM(message, BF16),
            pltpu.VMEM(message, BF16),
            pltpu.VMEM(message, BF16),
            pltpu.SemaphoreType.DMA((5,)),
            pltpu.SemaphoreType.DMA((3,)),
            pltpu.SemaphoreType.DMA((3, 3)),
            pltpu.SemaphoreType.DMA((3, 3)),
        ],
        compiler_params=pltpu.CompilerParams(
            collective_id=0, has_side_effects=True, vmem_limit_bytes=32 * 1024 * 1024
        ),
    )(
        block_brick.reshape(1, -1),
        brick_slot.reshape(1, -1),
        counts.reshape(1, -1),
        grid_fields,
        node_mask,
        part_mass,
        shape_t.reshape(blocks * NODES, PBLK),
        part_vel.transpose(1, 0, 2),
    )
    return vel.transpose(1, 0, 2), momentum


def solution(mesh):
    placed = (
        P(("col", "grp"), None),
        P("col"),
        P(("col", "grp")),
        P(("col", "grp"), None),
        P(("col", "grp")),
        P(("col", "grp"), None, None),
        P(("col", "grp"), None),
        P(("col", "grp"), None, None),
    )
    return jax.shard_map(
        functools.partial(local, mesh.shape["col"]),
        mesh=mesh,
        in_specs=placed,
        out_specs=(P(("col", "grp"), None, None), P(("col", "grp"), None)),
        check_vma=False,
    )
```

time: 106 us -> 27.4 us (0.26); the launches traced: 104 us -> 26.9 us
  blocking collectives: 70.3 us -> 0 us
  Pallas kernels: 0 us -> 20.3 us
  starting transfers between devices: 19.6 us -> 0 us
  local copies, waits for them, and re-layouts: 8.86 us -> 5.94 us
  matrix products: 2.29 us -> 0 us
  other arithmetic: 2.28 us -> 0 us
    psum x1 -> x0, blocking collectives: 37.6 us -> none  [local(): totals = lax.psum(edge_in, 'grp')]
    all_gather x1 -> x0, blocking collectives: 32.7 us -> none  [local(): gathered = lax.all_gather(grid_fields, 'grp', axis=0, tiled=True)]
    pallas_call x0 -> x1, Pallas kernels: none -> 20.3 us  [local(): pl.pallas_call(functools.partial(kernel, ncols, groups, slots), out_shape...]
    all_to_all x2 -> x0, starting transfers between devices: 11.3 us -> none  [the longest x1 5.72 us: local(): lax.all_to_all(send_rows.reshape(groups, slots_each, OUTF * NODES), 'grp'...]
    ppermute x4 -> x0, starting transfers between devices: 8.35 us -> none  [the longest x2 5.77 us: with_halo(): lax.ppermute(tail, axis, [(i, (i + 1) % count) for i in range(ends)])]
    unnamed x15 -> x18, local copies, waits for them, and re-layouts: 2.12 us -> 5.94 us
    gather x5 -> x0, local copies, waits for them, and re-layouts: 3.3 us -> none  [the longest x1 1.15 us: local(): logical = jnp.take(gathered, brick_slot, axis=0)]
    dot_general x5 -> x0, matrix products: 2.29 us -> none  [the longest x1 0.89 us: local(): jnp.dot(edge_match.astype(jnp.float32).T, totals, precision=lax.Precision...]
  transfers between devices with their start and end apart: 6 -> 0, of which waited for: 0 -> 0; matrix products, arithmetic and copies ran while one was open for 8% -> 0% of each run, Pallas kernels for 0% -> 0%
where the time goes in v1:
time: 27.4 us; the launch traced here: 26.9 us
  Pallas kernels  20.3 us (74%)
  local copies, waits for them, and re-layouts  5.94 us (22%)
  between operations  0.67 us (2%)
    pallas_call x1, Pallas kernels, local(): pl.pallas_call(functools.partial(kernel, ncols, groups, slots), out_shape...  20.3 us
    unnamed x18, local copies, waits for them, and re-layouts  5.94 us

profile of v1, /device:TPU:0, one launch (start us, length us, event | category | flops | bytes accessed | tf_op | source)
XLA Modules:
  0.0 26.9 jit_solution(5212084999713530199)
XLA Ops:
  0.6 0.0 copy-start.7
  0.6 0.0 copy-start.5
  0.7 0.0 copy-start.6
  0.7 0.6 %copy-done.7 = s32[32]{0:T(128)S(1)} copy-done((s32[32]{0:T(128)S(1)}, s32[32]{0:T(128)}, u32[]{:S(2)}) %copy-start.7) | copy-done | bytes 152
  1.3 0.0 copy-done.5
  1.3 0.0 copy-done.6
  1.3 0.0 copy-start
  1.3 1.0 %copy-done = bf16[32,64,128]{2,1,0:T(8,128)(2,1)S(1)} copy-done((bf16[32,64,128]{2,1,0:T(8,128)(2,1)S(1)}, bf16[32,64,128]{2,1,0:T(8,128)(2,1)}, u32[]{:S(2)}) %copy-start) | copy-done | bytes 524312
  2.4 0.0 copy-start.1
  2.4 0.8 %copy-done.1 = f32[32,3,128]{2,0,1:T(8,128)S(1)} copy-done((f32[32,3,128]{2,0,1:T(8,128)S(1)}, f32[32,3,128]{2,0,1:T(8,128)}, u32[]{:S(2)}) %copy-start.1) | copy-done | bytes 49176
  3.2 0.0 copy-start.2
  3.2 0.8 %copy-done.2 = bf16[32,512]{1,0:T(8,128)(2,1)S(1)} copy-done((bf16[32,512]{1,0:T(8,128)(2,1)S(1)}, bf16[32,512]{1,0:T(8,128)(2,1)}, u32[]{:S(2)}) %copy-start.2) | copy-done | bytes 32792
  3.9 0.0 copy-start.3
  3.9 0.7 %copy-done.3 = s32[32,64]{1,0:T(8,128)S(1)} copy-done((s32[32,64]{1,0:T(8,128)S(1)}, s32[32,64]{1,0:T(8,128)}, u32[]{:S(2)}) %copy-start.3) | copy-done | bytes 8216
  4.6 0.0 copy-start.4
  4.7 0.7 %copy-done.4 = f32[32,128]{1,0:T(8,128)S(1)} copy-done((f32[32,128]{1,0:T(8,128)S(1)}, f32[32,128]{1,0:T(8,128)}, u32[]{:S(2)}) %copy-start.4) | copy-done | bytes 16408
  5.4 20.3 %shard_map.95 = (f32[3,32,128]{2,1,0:T(8,128)S(1)}, f32[32,256]{1,0:T(8,128)S(1)}) custom-call(s32[1,32]{1,0:T(1,128)S(1)} %bitcast.10, s32[1,256]{1,0:T(1,128)S(1)} %bitcast.9, s32[1,32]{1,0:T(1,128)S(1)} %bitcast.11, bf16[32,512]{1,0:T(8,128)(2,1)S(1)} %copy-done.2, s32[32,64]{1,0:T(8,128)S(1)} %copy-done.3, f32[32,128]{1,0:T(8,128)S(1)} %copy-done.4, ...), custom_call_target="tpu_custom_call" | custom-call | tf_op jit(solution)/shard_map/pallas_call | solution.py:307
  25.7 0.6 %copy.12 = f32[32,3,128]{2,0,1:T(8,128)} copy(f32[32,3,128]{2,0,1:T(8,128)S(1)} %bitcast.8) | data formatting | bytes 98304
  26.3 0.6 %copy.13 = f32[32,256]{1,0:T(8,128)} copy(f32[32,256]{1,0:T(8,128)S(1)} %get-tuple-element.9) | data formatting | bytes 65536
Async XLA Ops:
  0.6 0.7 %copy-start.7 = (s32[32]{0:T(128)S(1)}, s32[32]{0:T(128)}, u32[]{:S(2)}) copy-start(s32[32]{0:T(128)} %param.12) | copy-start | bytes 388
  0.6 0.7 %copy-start.5 = (s32[256]{0:T(256)S(1)}, s32[256]{0:T(256)}, u32[]{:S(2)}) copy-start(s32[256]{0:T(256)} %param.9) | copy-start | bytes 3076
  0.7 0.7 %copy-start.6 = (s32[32]{0:T(128)S(1)}, s32[32]{0:T(128)}, u32[]{:S(2)}) copy-start(s32[32]{0:T(128)} %param.10) | copy-start | bytes 388
  1.3 1.0 %copy-start = (bf16[32,64,128]{2,1,0:T(8,128)(2,1)S(1)}, bf16[32,64,128]{2,1,0:T(8,128)(2,1)}, u32[]{:S(2)}) copy-start(bf16[32,64,128]{2,1,0:T(8,128)(2,1)} %param.13) | copy-start | bytes 1572868
  2.4 0.8 %copy-start.1 = (f32[32,3,128]{2,0,1:T(8,128)S(1)}, f32[32,3,128]{2,0,1:T(8,128)}, u32[]{:S(2)}) copy-start(f32[32,3,128]{2,0,1:T(8,128)} %param.15) | copy-start | bytes 147460
  3.2 0.8 %copy-start.2 = (bf16[32,512]{1,0:T(8,128)(2,1)S(1)}, bf16[32,512]{1,0:T(8,128)(2,1)}, u32[]{:S(2)}) copy-start(bf16[32,512]{1,0:T(8,128)(2,1)} %grid_in.1) | copy-start | bytes 98308
  3.9 0.7 %copy-start.3 = (s32[32,64]{1,0:T(8,128)S(1)}, s32[32,64]{1,0:T(8,128)}, u32[]{:S(2)}) copy-start(s32[32,64]{1,0:T(8,128)} %mask_in.1) | copy-start | bytes 24580
  4.6 0.7 %copy-start.4 = (f32[32,128]{1,0:T(8,128)S(1)}, f32[32,128]{1,0:T(8,128)}, u32[]{:S(2)}) copy-start(f32[32,128]{1,0:T(8,128)} %mass_in.1) | copy-start | bytes 49156

commit v2 on v1

--- a/solution.py
+++ b/solution.py
@@ -25,9 +25,9 @@
 
 def kernel(
     ncols, groups, slots,
-    bb_ref, slot_ref, cnt_ref, grid_in, mask_in, mass_in, w_in, pv_in,
-    vel_ref, mom_ref,
-    grid_v, mask_v, mass_v, w_v, pv_v,
+    bb_in, slot_in, cnt_in, grid_in, mask_in, mass_in, w_in, pv_in,
+    vel_ref, place_ref, arrived_ref,
+    bb_ref, slot_ref, cnt_ref, grid_v, mask_v, mass_v, w_v, pv_v,
     req_out, edge_out, req_in, f_out, f_in, p_out, p_in,
     in_sem, self_sem, send_sem, recv_sem,
 ):
@@ -61,15 +61,20 @@
             pl.semaphore_signal(barrier, inc=1, device_id=(c + dc, d), device_id_type=MESH)
         return go
 
-    peers(greet(0), greet(-1), greet(1))
     loads = [
         pltpu.make_async_copy(src, dst, in_sem.at[i])
         for i, (src, dst) in enumerate(
-            ((grid_in, grid_v), (mask_in, mask_v), (mass_in, mass_v), (pv_in, pv_v), (w_in, w_v))
+            (
+                (grid_in, grid_v), (mask_in, mask_v), (mass_in, mass_v), (pv_in, pv_v), (w_in, w_v),
+                (bb_in, bb_ref), (slot_in, slot_ref), (cnt_in, cnt_ref),
+            )
         )
     ]
-    for load in loads:
-        load.start()
+    for i in (5, 6, 7, 0, 1, 4, 2, 3):
+        loads[i].start()
+    peers(greet(0), greet(-1), greet(1))
+    loads[5].wait()
+    loads[6].wait()
 
     bb = bb_ref[...].astype(F32)
     slotf = slot_ref[...].astype(F32)
@@ -177,6 +182,7 @@
     edge_high = jnp.sum(
         jnp.where(edge_lane == edge_sub + (columns - RIM), slotf, 0.0), axis=1, keepdims=True
     )
+    loads[7].wait()
     cnt_col = to_col(cnt_ref[...].astype(F32))
     loads[0].wait()
     grid = grid_v[...]
@@ -217,9 +223,9 @@
     f_out[...] = across(pack, grid_stack)
     exchange(1, lambda sec, d: f_out.at[sec * groups + d], f_in)
 
-    place = [
-        (pieces[t] + pieces[t + 2]).astype(BF16) for t in range(2)
-    ]
+    place_ref[...] = jnp.concatenate(
+        [pieces[t] + pieces[t + 2] for t in range(2)], axis=0
+    ).astype(BF16)
     loads[2].wait()
     loads[3].wait()
     loads[4].wait()
@@ -284,12 +290,21 @@
     sent(0, req_in)
     sent(1, f_in)
     arrive(2, p_in)
-    arrived = p_in[...].reshape(3 * width, LANES)
+    arrived_ref[...] = p_in[...].reshape(3 * width, LANES)
+    sent(2, p_in)
+
+
+def finish(vel_in, place_in, arrived_in, vel_out, mom_out, mom_v, sem):
+    rows = mom_out.shape[0]
+    save = pltpu.make_async_copy(vel_in, vel_out, sem.at[0])
+    save.start()
+    both = jnp.dot(place_in[...], arrived_in[...], preferred_element_type=F32)
     for t in range(2):
-        mom_ref[:, t * LANES : (t + 1) * LANES] = jnp.dot(
-            place[t], arrived, preferred_element_type=F32
-        )
-    sent(2, p_in)
+        mom_v[:, t * LANES : (t + 1) * LANES] = both[t * rows : (t + 1) * rows]
+    store = pltpu.make_async_copy(mom_v, mom_out, sem.at[1])
+    store.start()
+    save.wait()
+    store.wait()
 
 
 def local(ncols, grid_fields, brick_slot, block_brick, node_mask, counts, shape_t, part_mass, part_vel):
@@ -302,17 +317,21 @@
         slots *= 2
     width = groups * PIECES * slots
     vmem = pl.BlockSpec(memory_space=pltpu.VMEM)
-    hbm = pl.BlockSpec(memory_space=pl.ANY)
+    hbm = pl.BlockSpec(memory_space=pltpu.HBM)
     message = (3 * groups, PIECES * slots, LANES)
-    vel, momentum = pl.pallas_call(
+    vel, place, arrived = pl.pallas_call(
         functools.partial(kernel, ncols, groups, slots),
         out_shape=(
             jax.ShapeDtypeStruct((3, blocks, PBLK), F32),
-            jax.ShapeDtypeStruct((rows, OUTF * NODES), F32),
+            jax.ShapeDtypeStruct((2 * rows, 3 * width), BF16),
+            jax.ShapeDtypeStruct((3 * width, LANES), BF16),
         ),
-        in_specs=[vmem] * 3 + [hbm] * 5,
-        out_specs=(vmem, vmem),
+        in_specs=[hbm] * 8,
+        out_specs=(vmem, vmem, vmem),
         scratch_shapes=[
+            pltpu.VMEM((1, blocks), jnp.int32),
+            pltpu.VMEM((1, brick_slot.shape[0]), jnp.int32),
+            pltpu.VMEM((1, blocks), jnp.int32),
             pltpu.VMEM(grid_fields.shape, BF16),
             pltpu.VMEM(node_mask.shape, jnp.int32),
             pltpu.VMEM(part_mass.shape, F32),
@@ -325,13 +344,13 @@
             pltpu.VMEM(message, BF16),
             pltpu.VMEM(message, BF16),
             pltpu.VMEM(message, BF16),
-            pltpu.SemaphoreType.DMA((5,)),
+            pltpu.SemaphoreType.DMA((8,)),
             pltpu.SemaphoreType.DMA((3,)),
             pltpu.SemaphoreType.DMA((3, 3)),
             pltpu.SemaphoreType.DMA((3, 3)),
         ],
         compiler_params=pltpu.CompilerParams(
-            collective_id=0, has_side_effects=True, vmem_limit_bytes=32 * 1024 * 1024
+            collective_id=0, has_side_effects=True
         ),
     )(
         block_brick.reshape(1, -1),
@@ -343,6 +362,19 @@
         shape_t.reshape(blocks * NODES, PBLK),
         part_vel.transpose(1, 0, 2),
     )
+    vel, momentum = pl.pallas_call(
+        finish,
+        out_shape=(
+            jax.ShapeDtypeStruct((3, blocks, PBLK), F32),
+            jax.ShapeDtypeStruct((rows, OUTF * NODES), F32),
+        ),
+        in_specs=[vmem] * 3,
+        out_specs=(hbm, hbm),
+        scratch_shapes=[
+            pltpu.VMEM((rows, OUTF * NODES), F32),
+            pltpu.SemaphoreType.DMA((2,)),
+        ],
+    )(vel, place, arrived)
     return vel.transpose(1, 0, 2), momentum
 
 

time: 27.4 us -> 23.4 us (0.85); the launches traced: 26.9 us -> 23.3 us
  local copies, waits for them, and re-layouts: 5.94 us -> 0 us
  Pallas kernels: 20.3 us -> 22.6 us
    unnamed x18 -> x0, local copies, waits for them, and re-layouts: 5.94 us -> none
    pallas_call x0 -> x1, Pallas kernels: none -> 1.73 us  [local(): pl.pallas_call(finish, out_shape=(jax.ShapeDtypeStruct((3, blocks, PBLK),...]
    pallas_call x1, Pallas kernels: 20.3 us -> 20.9 us  [local(): pl.pallas_call(functools.partial(kernel, ncols, groups, slots), out_shape...]
where the time goes in v2:
time: 23.4 us; the launch traced here: 23.3 us
  Pallas kernels  22.6 us (97%)
  between operations  0.64 us (3%)
    pallas_call x1, Pallas kernels, local(): pl.pallas_call(functools.partial(kernel, ncols, groups, slots), out_shape...  20.9 us
    pallas_call x1, Pallas kernels, local(): pl.pallas_call(finish, out_shape=(jax.ShapeDtypeStruct((3, blocks, PBLK),...  1.73 us

profile of v2, /device:TPU:0, one launch (start us, length us, event | category | flops | bytes accessed | tf_op | source)
XLA Modules:
  0.0 23.3 jit_solution(14539898335920298568)
XLA Ops:
  0.6 20.9 %shard_map.95 = (f32[3,32,128]{2,1,0:T(8,128)}, bf16[64,384]{1,0:T(8,128)(2,1)}, bf16[384,128]{1,0:T(8,128)(2,1)}) custom-call(s32[1,32]{1,0:T(1,128)} %bitcast.9, s32[1,256]{1,0:T(1,128)} %bitcast.8, s32[1,32]{1,0:T(1,128)} %bitcast.10, bf16[32,512]{1,0:T(8,128)(2,1)} %grid_in.1, s32[32,64]{1,0:T(8,128)} %mask_in.1, f32[32,128]{1,0:T(8,128)} %mass_in.1, ...), custom_call_target="tpu_custom_call" | custom-call | tf_op jit(solution)/shard_map/pallas_call | solution.py:322
  21.5 1.7 %shard_map.96 = (f32[3,32,128]{2,1,0:T(8,128)}, f32[32,256]{1,0:T(8,128)}) custom-call(f32[3,32,128]{2,1,0:T(8,128)} %get-tuple-element.7.vel_in, bf16[64,384]{1,0:T(8,128)(2,1)} %get-tuple-element.8.place_in, bf16[384,128]{1,0:T(8,128)(2,1)} %get-tuple-element.9.arrived_in), custom_call_target="tpu_custom_call" | custom-call | tf_op jit(solution)/shard_map/pallas_call | solution.py:365

commit v3 on v2

--- a/solution.py
+++ b/solution.py
@@ -26,7 +26,7 @@
 def kernel(
     ncols, groups, slots,
     bb_in, slot_in, cnt_in, grid_in, mask_in, mass_in, w_in, pv_in,
-    vel_ref, place_ref, arrived_ref,
+    vel_ref, mom_ref,
     bb_ref, slot_ref, cnt_ref, grid_v, mask_v, mass_v, w_v, pv_v,
     req_out, edge_out, req_in, f_out, f_in, p_out, p_in,
     in_sem, self_sem, send_sem, recv_sem,
@@ -42,19 +42,27 @@
     barrier = pltpu.get_barrier_semaphore()
 
     def peers(body_own, body_left, body_right):
+        upper = g >= groups // 2
+        first, way = jnp.where(upper, 0, groups - 1), jnp.where(upper, 1, -1)
+        self_at = (g - first) * way
+        half = groups // 2
+
         def own(i, carry):
-            body_own(lax.rem(g + i, groups))
+            body_own(first + way * jnp.where(i >= self_at, i + 1, i))
             return carry
 
-        def side(body):
+        def side(body, start, stop):
             def run(i, carry):
-                body(lax.rem(g + i, groups))
+                body(first + way * i)
                 return carry
-            lax.fori_loop(0, groups, run, 0, unroll=groups <= 8)
-
-        pl.when(has[0])(lambda: side(body_left))
-        pl.when(has[2])(lambda: side(body_right))
-        lax.fori_loop(1, groups, own, 0, unroll=groups <= 8)
+            lax.fori_loop(start, stop, run, 0, unroll=groups <= 8)
+
+        lax.fori_loop(0, half, own, 0, unroll=groups <= 8)
+        pl.when(has[0])(lambda: side(body_left, 0, half))
+        pl.when(has[2])(lambda: side(body_right, 0, half))
+        lax.fori_loop(half, groups - 1, own, 0, unroll=groups <= 8)
+        pl.when(has[0])(lambda: side(body_left, half, groups))
+        pl.when(has[2])(lambda: side(body_right, half, groups))
 
     def greet(dc):
         def go(d):
@@ -223,7 +231,7 @@
     f_out[...] = across(pack, grid_stack)
     exchange(1, lambda sec, d: f_out.at[sec * groups + d], f_in)
 
-    place_ref[...] = jnp.concatenate(
+    place = jnp.concatenate(
         [pieces[t] + pieces[t + 2] for t in range(2)], axis=0
     ).astype(BF16)
     loads[2].wait()
@@ -290,21 +298,21 @@
     sent(0, req_in)
     sent(1, f_in)
     arrive(2, p_in)
-    arrived_ref[...] = p_in[...].reshape(3 * width, LANES)
+    both = jnp.dot(place, p_in[...].reshape(3 * width, LANES), preferred_element_type=F32)
+    for t in range(2):
+        mom_ref[:, t * LANES : (t + 1) * LANES] = both[t * rows : (t + 1) * rows]
     sent(2, p_in)
 
 
-def finish(vel_in, place_in, arrived_in, vel_out, mom_out, mom_v, sem):
-    rows = mom_out.shape[0]
-    save = pltpu.make_async_copy(vel_in, vel_out, sem.at[0])
-    save.start()
-    both = jnp.dot(place_in[...], arrived_in[...], preferred_element_type=F32)
-    for t in range(2):
-        mom_v[:, t * LANES : (t + 1) * LANES] = both[t * rows : (t + 1) * rows]
-    store = pltpu.make_async_copy(mom_v, mom_out, sem.at[1])
-    store.start()
-    save.wait()
-    store.wait()
+def finish(vel_in, mom_in, vel_out, mom_out, sem):
+    saves = [
+        pltpu.make_async_copy(src, dst, sem.at[i])
+        for i, (src, dst) in enumerate(((vel_in, vel_out), (mom_in, mom_out)))
+    ]
+    for save in saves:
+        save.start()
+    for save in saves:
+        save.wait()
 
 
 def local(ncols, grid_fields, brick_slot, block_brick, node_mask, counts, shape_t, part_mass, part_vel):
@@ -319,15 +327,14 @@
     vmem = pl.BlockSpec(memory_space=pltpu.VMEM)
     hbm = pl.BlockSpec(memory_space=pltpu.HBM)
     message = (3 * groups, PIECES * slots, LANES)
-    vel, place, arrived = pl.pallas_call(
+    vel, momentum = pl.pallas_call(
         functools.partial(kernel, ncols, groups, slots),
         out_shape=(
-            jax.ShapeDtypeStruct((3, blocks, PBLK), F32),
-            jax.ShapeDtypeStruct((2 * rows, 3 * width), BF16),
-            jax.ShapeDtypeStruct((3 * width, LANES), BF16),
+            pltpu.VMEM((3, blocks, PBLK), F32),
+            pltpu.VMEM((rows, OUTF * NODES), F32),
         ),
         in_specs=[hbm] * 8,
-        out_specs=(vmem, vmem, vmem),
+        out_specs=(vmem, vmem),
         scratch_shapes=[
             pltpu.VMEM((1, blocks), jnp.int32),
             pltpu.VMEM((1, brick_slot.shape[0]), jnp.int32),
@@ -350,31 +357,36 @@
             pltpu.SemaphoreType.DMA((3, 3)),
         ],
         compiler_params=pltpu.CompilerParams(
-            collective_id=0, has_side_effects=True
+            collective_id=0, has_side_effects=True, vmem_limit_bytes=32 * 1024 * 1024
         ),
     )(
-        block_brick.reshape(1, -1),
-        brick_slot.reshape(1, -1),
-        counts.reshape(1, -1),
-        grid_fields,
-        node_mask,
-        part_mass,
-        shape_t.reshape(blocks * NODES, PBLK),
-        part_vel.transpose(1, 0, 2),
+        *(
+            pltpu.with_memory_space_constraint(x, pltpu.HBM)
+            for x in (
+                block_brick.reshape(1, -1),
+                brick_slot.reshape(1, -1),
+                counts.reshape(1, -1),
+                grid_fields,
+                node_mask,
+                part_mass,
+                shape_t.reshape(blocks * NODES, PBLK),
+                part_vel.transpose(1, 0, 2),
+            )
+        )
     )
     vel, momentum = pl.pallas_call(
         finish,
         out_shape=(
-            jax.ShapeDtypeStruct((3, blocks, PBLK), F32),
-            jax.ShapeDtypeStruct((rows, OUTF * NODES), F32),
+            pltpu.HBM((3, blocks, PBLK), F32),
+            pltpu.HBM((rows, OUTF * NODES), F32),
         ),
-        in_specs=[vmem] * 3,
+        in_specs=[vmem] * 2,
         out_specs=(hbm, hbm),
-        scratch_shapes=[
-            pltpu.VMEM((rows, OUTF * NODES), F32),
-            pltpu.SemaphoreType.DMA((2,)),
-        ],
-    )(vel, place, arrived)
+        scratch_shapes=[pltpu.SemaphoreType.DMA((2,))],
+    )(
+        pltpu.with_memory_space_constraint(vel, pltpu.VMEM),
+        pltpu.with_memory_space_constraint(momentum, pltpu.VMEM),
+    )
     return vel.transpose(1, 0, 2), momentum
 
 

time: 23.4 us -> 21.7 us (0.927)
  Pallas kernels: 22.6 us -> 20.9 us
    pallas_call x1, Pallas kernels: 1.73 us -> 0.65 us  [local(): pl.pallas_call(finish, out_shape=(pltpu.HBM((3, blocks, PBLK), F32), pltp...]
    pallas_call x1, Pallas kernels: 20.9 us -> 20.2 us  [local(): pl.pallas_call(functools.partial(kernel, ncols, groups, slots), out_shape...]
where the time goes in v3:
time: 21.7 us; the launch traced here: 21.5 us
  Pallas kernels  20.9 us (96%)
  between operations  0.64 us (3%)
    pallas_call x1, Pallas kernels, local(): pl.pallas_call(functools.partial(kernel, ncols, groups, slots), out_shape...  20.2 us
    pallas_call x1, Pallas kernels, local(): pl.pallas_call(finish, out_shape=(pltpu.HBM((3, blocks, PBLK), F32), pltp...  0.65 us

profile of v3, /device:TPU:0, one launch (start us, length us, event | category | flops | bytes accessed | tf_op | source)
XLA Modules:
  0.0 21.5 jit_solution(2342759492293210022)
XLA Ops:
  0.6 20.2 %shard_map.95 = (f32[3,32,128]{2,1,0:T(8,128)S(1)}, f32[32,256]{1,0:T(8,128)S(1)}) custom-call(s32[1,32]{1,0:T(1,128)} %bitcast.9, s32[1,256]{1,0:T(1,128)} %bitcast.8, s32[1,32]{1,0:T(1,128)} %bitcast.10, bf16[32,512]{1,0:T(8,128)(2,1)} %grid_in.1, s32[32,64]{1,0:T(8,128)} %mask_in.1, f32[32,128]{1,0:T(8,128)} %mass_in.1, bf16[2048,128]{1,0:T(8,128)(2,1)} %bitcast.6, ...), custom_call_target="tpu_custom_call" | custom-call | tf_op jit(solution)/shard_map/pallas_call | solution.py:330
  20.9 0.7 %shard_map.96 = (f32[3,32,128]{2,1,0:T(8,128)}, f32[32,256]{1,0:T(8,128)}) custom-call(f32[3,32,128]{2,1,0:T(8,128)S(1)} %get-tuple-element.6.vel_in, f32[32,256]{1,0:T(8,128)S(1)} %get-tuple-element.7.mom_in), custom_call_target="tpu_custom_call" | custom-call | tf_op jit(solution)/shard_map/pallas_call | solution.py:377

commit v4 on v3

--- a/solution.py
+++ b/solution.py
@@ -28,7 +28,7 @@
     bb_in, slot_in, cnt_in, grid_in, mask_in, mass_in, w_in, pv_in,
     vel_ref, mom_ref,
     bb_ref, slot_ref, cnt_ref, grid_v, mask_v, mass_v, w_v, pv_v,
-    req_out, edge_out, req_in, f_out, f_in, p_out, p_in,
+    req_out, edge_out, req_in, f_out, f_in, p_out, p_in, e_out, e_in,
     in_sem, self_sem, send_sem, recv_sem,
 ):
     blocks = bb_ref.shape[1]
@@ -157,8 +157,8 @@
             )
 
     def clear(sec):
-        for ref in (req_in, f_in, p_in):
-            part = ref.at[pl.ds(sec * groups, groups)]
+        for ref, at in ((req_in, sec), (f_in, sec), (e_in, sec // 2)):
+            part = ref.at[pl.ds(at * groups, groups)]
             part[...] = jnp.zeros(part.shape, ref.dtype)
 
     for sec in (0, 2):
@@ -294,14 +294,51 @@
     high = [x.astype(BF16) for x in partial]
     rest = [(x - h.astype(F32)).astype(BF16) for x, h in zip(partial, high)]
     p_out[...] = across(unpack, jnp.concatenate(high + rest, axis=0))
-    exchange(2, lambda sec, d: p_out.at[sec * groups + d], p_in)
+    for i in range(2):
+        e_out[i] = jnp.concatenate([x[i : i + 1] for x in partial], axis=1)
+
+    def deliver(sec):
+        def go(d):
+            pltpu.make_async_remote_copy(
+                src_ref=p_out.at[groups + d] if sec == 1 else e_out.at[sec // 2],
+                dst_ref=p_in.at[groups + g] if sec == 1 else e_in.at[(1 - sec // 2) * groups + g],
+                send_sem=send_sem.at[2, sec],
+                recv_sem=recv_sem.at[2, 2 - sec],
+                device_id=(c + sec - 1, d),
+                device_id_type=MESH,
+            ).start()
+        return go
+
+    peers(deliver(1), deliver(0), deliver(2))
+    pltpu.make_async_copy(p_out.at[groups + g], p_in.at[groups + g], self_sem.at[2]).start()
+
+    def edges(sem):
+        for sec in (0, 2):
+            pl.when(has[sec])(
+                lambda sec=sec: bytes_wait(e_in, sec // 2 * groups, groups, sem.at[2, sec])
+            )
+
     sent(0, req_in)
     sent(1, f_in)
-    arrive(2, p_in)
-    both = jnp.dot(place, p_in[...].reshape(3 * width, LANES), preferred_element_type=F32)
+    bytes_wait(p_in, groups, 1, self_sem.at[2])
+    bytes_wait(p_in, groups, groups - 1, recv_sem.at[2, 1])
+    edges(recv_sem)
+    both = jnp.dot(
+        place[:, width : 2 * width],
+        p_in[groups : 2 * groups].reshape(width, LANES),
+        preferred_element_type=F32,
+    )
+    row_id = iota((rows, OUTF * NODES), 0).astype(F32)
+    added = jnp.zeros((rows, OUTF * NODES), F32)
+    for k in range(2 * groups):
+        at = (k // groups * 2) * width + k % groups * PIECES * slots
+        added = added + jnp.where(row_id == want[:, at : at + 1], e_in[k], 0.0)
     for t in range(2):
-        mom_ref[:, t * LANES : (t + 1) * LANES] = both[t * rows : (t + 1) * rows]
-    sent(2, p_in)
+        mom_ref[:, t * LANES : (t + 1) * LANES] = (
+            both[t * rows : (t + 1) * rows] + added[:, t * LANES : (t + 1) * LANES]
+        )
+    bytes_wait(p_in, groups, groups - 1, send_sem.at[2, 1])
+    edges(send_sem)
 
 
 def finish(vel_in, mom_in, vel_out, mom_out, sem):
@@ -351,6 +388,8 @@
             pltpu.VMEM(message, BF16),
             pltpu.VMEM(message, BF16),
             pltpu.VMEM(message, BF16),
+            pltpu.VMEM((2, 1, OUTF * NODES), F32),
+            pltpu.VMEM((2 * groups, 1, OUTF * NODES), F32),
             pltpu.SemaphoreType.DMA((8,)),
             pltpu.SemaphoreType.DMA((3,)),
             pltpu.SemaphoreType.DMA((3, 3)),

time: 21.7 us -> 21.4 us (0.986)
  Pallas kernels: 20.9 us -> 20.4 us
    pallas_call x1, Pallas kernels: 20.2 us -> 19.8 us  [local(): pl.pallas_call(functools.partial(kernel, ncols, groups, slots), out_shape...]
where the time goes in v4:
time: 21.4 us; the launch traced here: 21.1 us
  Pallas kernels  20.4 us (95%)
  between operations  0.64 us (3%)
    pallas_call x1, Pallas kernels, local(): pl.pallas_call(functools.partial(kernel, ncols, groups, slots), out_shape...  19.8 us
    pallas_call x1, Pallas kernels, local(): pl.pallas_call(finish, out_shape=(pltpu.HBM((3, blocks, PBLK), F32), pltp...  0.65 us

profile of v4, /device:TPU:0, one launch (start us, length us, event | category | flops | bytes accessed | tf_op | source)
XLA Modules:
  0.0 21.1 jit_solution(14188071388797821759)
XLA Ops:
  0.6 19.8 %shard_map.95 = (f32[3,32,128]{2,1,0:T(8,128)S(1)}, f32[32,256]{1,0:T(8,128)S(1)}) custom-call(s32[1,32]{1,0:T(1,128)} %bitcast.9, s32[1,256]{1,0:T(1,128)} %bitcast.8, s32[1,32]{1,0:T(1,128)} %bitcast.10, bf16[32,512]{1,0:T(8,128)(2,1)} %grid_in.1, s32[32,64]{1,0:T(8,128)} %mask_in.1, f32[32,128]{1,0:T(8,128)} %mass_in.1, bf16[2048,128]{1,0:T(8,128)(2,1)} %bitcast.6, ...), custom_call_target="tpu_custom_call" | custom-call | tf_op jit(solution)/shard_map/pallas_call | solution.py:367
  20.4 0.7 %shard_map.96 = (f32[3,32,128]{2,1,0:T(8,128)}, f32[32,256]{1,0:T(8,128)}) custom-call(f32[3,32,128]{2,1,0:T(8,128)S(1)} %get-tuple-element.6.vel_in, f32[32,256]{1,0:T(8,128)S(1)} %get-tuple-element.7.mom_in), custom_call_target="tpu_custom_call" | custom-call | tf_op jit(solution)/shard_map/pallas_call | solution.py:416
